TPU v7x, 32 devices: a whole 2x2x4 slice. The times are simulated.
32 devices in a mesh: seq: 16 (over z, y, x), tp: 2 (over core).
Axes of the slice: x: 2, y: 2, z: 4, core: 2. Of those that a mesh axis runs over, the one named last changes fastest.
Arguments:
- query: bfloat16 [128, 2048], P('seq', 'tp'), may hold values from -8 to 8, as said below
- new_key: bfloat16 [128, 2048], P('seq', 'tp'), may hold values from -6 to 6
- new_value: bfloat16 [128, 2048], P('seq', 'tp'), may hold values from -6 to 6
- key_pool: bfloat16 [640, 64, 2048], P('seq', None, 'tp'), may hold values from -6 to 6
- value_pool: bfloat16 [640, 64, 2048], P('seq', None, 'tp'), may hold values from -6 to 6
- long_key: bfloat16 [4, 4096, 2048], P(None, 'seq', 'tp'), may hold values from -6 to 6
- long_value: bfloat16 [4, 4096, 2048], P(None, 'seq', 'tp'), may hold values from -6 to 6
- serve_table: int32 [160], P('seq'), may hold values from -1 to 127, as said below
- serve_len: int32 [160], P('seq'), may hold values from 0 to 256, as said below
- page_slot: int32 [640], P('seq'), may hold values from -1 to 9, as said below
- page_offset: int32 [640], P('seq'), may hold values from 0 to 192, as said below
- long_request: int32 [4], replicated, may hold values from 7 to 127, as said below
- long_len: int32 [4], replicated, may hold values from 2048 to 4096
- lambda_head: float32 [8], P('tp'), may hold values from 0.2 to 0.8
- norm_gain: float32 [2048], P('tp'), may hold values from 0.5 to 1.5
- out_weight: bfloat16 [2048, 2048], P('tp'), may hold values from -0.125 to 0.125
Outputs:
- layer_out: bfloat16 [128, 2048], P('seq', 'tp')
Inputs may be any that keep to these rules, and one draw needn't show every extreme that they name: `query`: rows r with r % 4 == 0 or r % 8 == 7 and all others follow the table's range. `serve_table`: every request that is not a long request stands in exactly one slot, possibly of another index of seq than its own; long requests stand in none; some index of seq fills all 10 slots. `serve_len`: the length of a request that stands in a slot is 1 or more. `page_slot`: A slot of length L owns exactly ceil(L / 64) pages of its own index of seq, with offsets 0, 64, 128 and so on; some index of seq uses all 40 pages. `page_offset`: free pages have offset 0. `long_request`: distinct request numbers.
All inputs are finite; a program needn't handle non-finite values.
Results may differ from a plain program's by a relative error of at most 0.019.
Values may be sent and summed in bfloat16 or wider, within the bound.
A program may use at most 64 MiB of HBM per device.

v0:
```python
import jax
import jax.numpy as jnp
from jax import lax
from jax.sharding import PartitionSpec as P

DH = 128
DV = 256
PG = 64


MASKED = -1e30


def page_terms(keys, values, page_q, live):
    page_count = keys.shape[0]
    cell_count = keys.shape[1]
    head_count = page_q.shape[1]
    shaped_keys = keys.reshape(page_count, cell_count, head_count, 2, DH)
    scores = jnp.einsum(
        "pchjd,phjd->pchj", shaped_keys, page_q, preferred_element_type=jnp.float32
    ) * DH ** (-0.5)
    live_mask = live[:, :, None, None]
    scores = jnp.where(live_mask, scores, MASKED)
    page_max = jnp.max(scores, axis=1)
    weights = jnp.where(live_mask, jnp.exp(scores - page_max[:, None]), 0.0)
    page_sum = jnp.sum(weights, axis=1)
    shaped_values = values.reshape(page_count, cell_count, head_count, DV)
    page_num = jnp.einsum(
        "pchj,pchv->phjv",
        weights.astype(jnp.bfloat16),
        shaped_values,
        preferred_element_type=jnp.float32,
    )
    return (page_max, page_sum, page_num)


def fold_pages(page_max, page_sum, page_num, owners, group_count):
    member = (owners[:, None] == jnp.arange(group_count)[None, :])[:, :, None, None]
    group_max = jnp.max(jnp.where(member, page_max[:, None], MASKED), axis=0)
    factor = jnp.where(
        member, jnp.exp(jnp.where(member, page_max[:, None] - group_max[None], 0.0)), 0.0
    )
    group_sum = jnp.einsum("pghj,phj->ghj", factor, page_sum, precision=lax.Precision.HIGHEST)
    group_num = jnp.einsum("pghj,phjv->ghjv", factor, page_num, precision=lax.Precision.HIGHEST)
    return (group_max, group_sum, group_num)


def on_device(
    query,
    new_key,
    new_value,
    key_pool,
    value_pool,
    long_key,
    long_value,
    serve_table,
    serve_len,
    page_slot,
    page_offset,
    long_request,
    long_len,
    lambda_head,
    norm_gain,
    out_weight,
):
    req_count = query.shape[0]
    head_count = lambda_head.shape[0]
    serve_count = serve_table.shape[0]
    long_count = long_request.shape[0]
    width = head_count * 2 * DV
    seq_index = lax.axis_index("seq")
    seq_count = lax.axis_size("seq")
    all_queries, all_served = (
        lax.all_gather(query, "seq", axis=0, tiled=True),
        lax.all_gather(serve_table, "seq", axis=0, tiled=True),
    )
    shaped_queries = all_queries.reshape(-1, head_count, 2, DH)
    slot_queries = shaped_queries[jnp.maximum(serve_table, 0)]
    safe_slot = jnp.maximum(page_slot, 0)
    cell_pos = page_offset[:, None] + jnp.arange(key_pool.shape[1])[None, :]
    live = (page_slot[:, None] >= 0) & (cell_pos < serve_len[safe_slot][:, None])
    pool_max, pool_sum, pool_num = page_terms(key_pool, value_pool, slot_queries[safe_slot], live)
    slot_max, slot_sum, slot_num = fold_pages(pool_max, pool_sum, pool_num, page_slot, serve_count)
    long_cells = long_key.shape[1]
    per_long = long_cells // PG
    long_pages = long_count * per_long
    long_queries = jnp.repeat(shaped_queries[long_request], per_long, axis=0)
    long_pos = seq_index * long_cells + jnp.arange(long_cells)
    long_live = (long_pos[None, :] < long_len[:, None]).reshape(long_pages, PG)
    part_max, part_sum, part_num = page_terms(
        long_key.reshape(long_pages, PG, -1),
        long_value.reshape(long_pages, PG, -1),
        long_queries,
        long_live,
    )
    long_owner = jnp.repeat(jnp.arange(long_count), per_long)
    long_max, long_sum, long_num = fold_pages(part_max, part_sum, part_num, long_owner, long_count)
    row_max, row_sum, row_num = (
        lax.all_gather(jnp.concatenate([slot_max, long_max], axis=0), "seq", axis=0, tiled=True),
        lax.all_gather(jnp.concatenate([slot_sum, long_sum], axis=0), "seq", axis=0, tiled=True),
        lax.all_gather(
            jnp.concatenate([slot_num, long_num], axis=0).reshape(-1, width),
            "seq",
            axis=0,
            tiled=True,
        ),
    )
    row_ids = jnp.concatenate(
        [
            all_served.reshape(seq_count, serve_count),
            jnp.broadcast_to(long_request[None, :], (seq_count, long_count)),
        ],
        axis=1,
    ).reshape(-1)
    row_num = row_num.reshape(-1, head_count, 2, DV)
    own_ids = seq_index * req_count + jnp.arange(req_count)
    member = (row_ids[None, :] == own_ids[:, None])[:, :, None, None]
    own_queries = query.reshape(req_count, head_count, 2, DH)
    own_keys = new_key.reshape(req_count, head_count, 2, DH)
    own_scores = jnp.einsum(
        "rhjd,rhjd->rhj", own_queries, own_keys, preferred_element_type=jnp.float32
    ) * DH ** (-0.5)
    best = jnp.maximum(own_scores, jnp.max(jnp.where(member, row_max[None], MASKED), axis=1))
    factor = jnp.where(member, jnp.exp(jnp.where(member, row_max[None] - best[:, None], 0.0)), 0.0)
    own_weight = jnp.exp(own_scores - best)
    denom = own_weight + jnp.einsum(
        "rnhj,nhj->rhj", factor, row_sum, precision=lax.Precision.HIGHEST
    )
    numer = own_weight[..., None] * new_value.reshape(req_count, head_count, 1, DV).astype(
        jnp.float32
    )
    numer = numer + jnp.einsum("rnhj,nhjv->rhjv", factor, row_num, precision=lax.Precision.HIGHEST)
    attn = numer / denom[..., None]
    diff = attn[:, :, 0] - lambda_head[None, :, None] * attn[:, :, 1]
    normed = (
        diff
        * lax.rsqrt(jnp.mean(diff * diff, axis=-1, keepdims=True) + 1e-05)
        * norm_gain.reshape(head_count, DV)
    )
    normed = normed.astype(jnp.bfloat16).reshape(req_count, head_count * DV)
    partial_out = jnp.dot(normed, out_weight, preferred_element_type=jnp.float32)
    return lax.psum_scatter(partial_out.astype(jnp.bfloat16), "tp", scatter_dimension=1, tiled=True)


def solution(mesh):
    return jax.shard_map(
        on_device,
        mesh=mesh,
        in_specs=(
            P("seq", "tp"),
            P("seq", "tp"),
            P("seq", "tp"),
            P("seq", None, "tp"),
            P("seq", None, "tp"),
            P(None, "seq", "tp"),
            P(None, "seq", "tp"),
            P("seq"),
            P("seq"),
            P("seq"),
            P("seq"),
            P(),
            P(),
            P("tp"),
            P("tp"),
            P("tp", None),
        ),
        out_specs=P("seq", "tp"),
        check_vma=False,
    )
```

profile of v0, /device:TPU:1, one launch (start us, length us, event | category | flops | bytes accessed | tf_op | source)
XLA Modules:
  0.0 204.2 jit_solution(1769684854029658026)
XLA Ops:
  6.5 0.7 broadcast_maximum_fusion.1
  7.2 0.7 broadcast_compare_fusion.2
  7.9 0.7 iota_compare_fusion
  8.5 0.7 broadcast_maximum_fusion
  9.2 0.7 compare_select_fusion
  9.9 0.7 lt.45
  10.6 0.1 lt.46
  10.7 0.1 eq.78
  10.8 36.2 %all_gather.16 = bf16[128,1024]{1,0:T(8,128)(2,1)S(1)} all-gather(bf16[8,1024]{1,0:T(8,128)(2,1)} %param.16), channel_id=1, replica_groups=mesh['seq'=16,'tp'=2] {'seq'}, dimensions={0}, use_global_device_ids=true | all-gather | bytes 278528 | tf_op jit(solution)/shard_map/all_gather | solution.py:74
  47.0 0.2 reshape.225
  47.1 0.6 gather_fusion.3
  47.7 0.6 gather_fusion.1
  48.3 0.8 gather_fusion
  49.1 0.7 gather_fusion.2
  49.8 4.4 %reshape_reshape.6 = bf16[16,64,4,2,128]{4,3,2,1,0:T(2,128)(2,1)} reshape(bf16[4,256,1024]{2,1,0:T(8,128)(2,1)} %param.21) | data formatting | bytes 4194304 | tf_op jit(solution)/shard_map/reshape;reshape | solution.py:18
  54.3 0.1 broadcast_compare_fusion
  54.4 2.9 %fusion.5 = f32[16,4,2,1,64]{4,3,2,1,0:T(1,128)S(1)} fusion(bf16[16,64,4,2,128]{4,3,2,1,0:T(2,128)(2,1)} %reshape_reshape.6, bf16[16,4,2,128,1]{3,2,1,0,4:T(2,128)(2,1)S(1)} %bitcast.106), kind=kOutput, calls=%fused_computation.10 | convolution fusion | flops 2097152 | bytes 2162688 | tf_op jit(solution)/shard_map/pchjd,phjd->pchj/dot_general | solution.py:19
  57.3 0.2 bitcast_reduce_fusion.1
  57.5 0.1 copy.52
  57.6 2.8 %reshape_reshape.7 = bf16[16,64,4,256]{3,2,1,0:T(4,128)(2,1)} reshape(bf16[4,256,1024]{2,1,0:T(8,128)(2,1)S(1)} %copy-done.1) | data formatting | bytes 4194304 | tf_op jit(solution)/shard_map/reshape;reshape | solution.py:27
  60.4 2.0 fusion.7
  62.4 9.4 %reshape.226 = bf16[40,64,4,2,128]{4,3,2,1,0:T(2,128)(2,1)} reshape(bf16[40,64,1024]{2,1,0:T(8,128)(2,1)} %param.19) | data formatting | bytes 10485760 | tf_op jit(solution)/shard_map/reshape | solution.py:18
  71.8 5.3 %fusion.3 = f32[40,4,2,1,64]{4,3,2,1,0:T(1,128)S(1)} fusion(bf16[40,64,4,2,128]{4,3,2,1,0:T(2,128)(2,1)} %reshape.226, bf16[40,4,2,128,1]{3,2,1,0,4:T(2,128)(2,1)S(1)} %bitcast.104), kind=kOutput, calls=%fused_computation.7 | convolution fusion | flops 5242880 | bytes 5406720 | tf_op jit(solution)/shard_map/pchjd,phjd->pchj/dot_general | solution.py:19
  77.1 0.1 fusion.51
  77.2 0.3 bitcast_reduce_fusion
  77.5 0.1 copy.51
  77.6 3.4 %fusion = f32[40,4,2,256]{3,2,1,0:T(2,128)S(1)} fusion(bf16[40,8,4,8,256]{4,3,2,1,0:T(8,128)(2,1)} %bitcast.114, pred[40,64]{1,0:T(8,128)(4,1)S(1)} %fusion.51, f32[40,4,2,64]{3,2,1,0:T(2,128)S(1)} %bitcast.94, f32[40,4,2]{2,1,0:T(4,128)S(1)} %bitcast_reduce_fusion), kind=kOutput, calls=%fused_computation.4 | convolution fusion | flops 10588160 | bytes 5656320 | tf_op jit(solution)/shard_map/pchj,pchv->phjv/dot_general | solution.py:28
  81.1 0.1 select_reduce_fusion.2
  81.2 0.3 convolution_bitcast_fusion.1
  81.4 0.1 select_reduce_fusion.1
  81.5 0.4 convolution_bitcast_fusion
  82.0 0.1 copy.59
  82.1 0.7 reshape.271
  82.9 0.1 pad.7.clone
  83.0 0.1 broadcast_bitcast_fusion
  83.1 0.6 dynamic-slice
  84.3 0.2 dynamic-update-slice
  84.6 5.3 %all-reduce = s32[160]{0:T(256)S(1)} all-reduce(s32[160]{0:T(256)S(1)} %dynamic-update-slice), channel_id=1, replica_groups=mesh['seq'=16,'tp'=2] {'seq'}, use_global_device_ids=true, to_apply=%add | all-reduce | flops 160 | bytes 1280
  89.8 0.1 reshape.224
  89.9 0.1 eq.71
  90.1 0.3 fusion.69
  90.4 0.1 copy.75
  90.5 0.3 fusion.54
  90.7 0.1 pad_maximum_fusion.1
  90.8 0.1 copy.53
  90.9 0.6 fusion.71
  91.5 0.1 copy.73
  91.6 0.3 fusion.30
  91.9 0.1 pad_maximum_fusion.2
  92.0 0.1 copy.61
  92.1 35.5 %all_gather.19 = f32[224,4,2]{1,2,0:T(2,128)S(1)} all-gather(f32[14,4,2]{1,2,0:T(2,128)S(1)} %copy.61), channel_id=1, replica_groups=mesh['seq'=16,'tp'=2] {'seq'}, dimensions={0}, use_global_device_ids=true | all-gather | bytes 7616 | tf_op jit(solution)/shard_map/all_gather | solution.py:100
  127.6 0.1 copy.77
  127.7 30.4 %all_gather.17 = f32[224,4,2]{1,2,0:T(2,128)S(1)} all-gather(f32[14,4,2]{1,2,0:T(2,128)S(1)} %copy.53), channel_id=1, replica_groups=mesh['seq'=16,'tp'=2] {'seq'}, dimensions={0}, use_global_device_ids=true | all-gather | bytes 7616 | tf_op jit(solution)/shard_map/all_gather | solution.py:99
  158.1 0.1 copy.54
  158.2 0.1 broadcast_compare_fusion.1
  158.3 0.1 select_reduce_fusion
  158.4 0.1 fusion.33
  158.5 0.3 fusion.29
  158.9 2.9 %reshape.230 = f32[224,4,2,256]{3,2,1,0:T(2,128)S(1)} reshape(f32[16,14,2048]{2,1,0:T(8,128)} %all-gather.3.cloned.1.call-done) | data formatting | bytes 3670016 | tf_op jit(solution)/shard_map/reshape | solution.py:115
  161.8 1.5 fusion.17
  163.3 0.2 fusion.32
  163.5 0.1 mul.97
  163.6 3.5 %convolution_convert_fusion = bf16[8,2048]{1,0:T(8,128)(2,1)} fusion(bf16[1024,2048]{1,0:T(8,128)(2,1)} %param.31, f32[8,1024]{1,0:T(8,128)S(1)} %bitcast.100, f32[8,1024]{1,0:T(8,128)S(1)} %bitcast.102, f32[8,1024]{1,0:T(8,128)S(1)} %bitcast.101, f32[1024]{0:T(1024)S(1)} %copy-done.5, f32[1024]{0:T(1024)S(1)} %bitcast.112), kind=kOutput, calls=%fused_computation.9 | convolution fusion | flops 33611776 | bytes 4333568 | tf_op jit(solution)/shard_map/dot_general | solution.py:141
  167.0 30.3 %reduce-scatter.2.cloned.1.call-done = bf16[8,1024]{1,0:T(8,128)(2,1)} async-done(((bf16[8,2048]{1,0:T(8,128)(2,1)}), bf16[8,1024]{1,0:T(8,128)(2,1)}) %reduce-scatter.2.cloned.1.call-update) | async-done | bytes 16400 | tf_op jit(solution)/shard_map/reduce_scatter | solution.py:142
  (47 shorter events, 0.3 us)
Async XLA Ops:
  6.5 41.8 %copy-start = (s32[10]{0:T(128)S(1)}, s32[10]{0:T(128)}, u32[]{:S(2)}) copy-start(s32[10]{0:T(128)} %param.24) | copy-start | bytes 124
  6.5 152.3 %all-gather.3.cloned.1.call-start = ((), (), s32[]{:S(2)}) async-start(), calls=%async_computation.2 | async-start | bytes 2228224 | tf_op jit(solution)/shard_map/all_gather | solution.py:101
  54.3 3.3 %copy-start.1 = (bf16[4,256,1024]{2,1,0:T(8,128)(2,1)S(1)}, bf16[4,256,1024]{2,1,0:T(8,128)(2,1)}, u32[]{:S(2)}) copy-start(bf16[4,256,1024]{2,1,0:T(8,128)(2,1)} %param.22) | copy-start | bytes 6291460
  71.8 5.3 %copy-start.7 = (s32[40]{0:T(128)S(1)}, s32[40]{0:T(128)}, u32[]{:S(2)}) copy-start(s32[40]{0:T(128)} %param.26) | copy-start | bytes 484
  77.6 5.3 %copy-start.8 = (s32[4]{0:T(128)S(1)}, s32[4]{0:T(128)}, u32[]{:S(2)}) copy-start(s32[4]{0:T(128)} %param.27) | copy-start | bytes 52
  77.6 5.4 %copy-start.6 = (f32[4]{0:T(128)S(1)}, f32[4]{0:T(128)}, u32[]{:S(2)}) copy-start(f32[4]{0:T(128)} %param.29) | copy-start | bytes 52
  77.6 5.5 %copy-start.10 = (u32[32]{0:T(128)S(1)}, u32[32]{0:T(128)}, u32[]{:S(2)}) copy-start(u32[32]{0:T(128)} %constant.49) | copy-start | bytes 388
  77.6 6.7 %copy-start.9 = (s32[10]{0:T(128)S(1)}, s32[10]{0:T(128)}, u32[]{:S(2)}) copy-start(s32[10]{0:T(128)} %param.23) | copy-start | bytes 124
  77.6 12.4 %copy-start.3 = (bf16[8,1024]{1,0:T(8,128)(2,1)S(1)}, bf16[8,1024]{1,0:T(8,128)(2,1)}, u32[]{:S(2)}) copy-start(bf16[8,1024]{1,0:T(8,128)(2,1)} %param.18) | copy-start | bytes 49156
  81.1 77.4 %copy-start.2 = (bf16[8,1024]{1,0:T(8,128)(2,1)S(1)}, bf16[8,1024]{1,0:T(8,128)(2,1)}, u32[]{:S(2)}) copy-start(bf16[8,1024]{1,0:T(8,128)(2,1)} %param.16) | copy-start | bytes 49156
  81.1 77.4 %copy-start.4 = (bf16[8,1024]{1,0:T(8,128)(2,1)S(1)}, bf16[8,1024]{1,0:T(8,128)(2,1)}, u32[]{:S(2)}) copy-start(bf16[8,1024]{1,0:T(8,128)(2,1)} %param.17) | copy-start | bytes 49156
  82.8 114.5 %reduce-scatter.2.cloned.1.call-start = ((), (), s32[]{:S(2)}) async-start(), calls=%async_computation.1 | async-start | bytes 49152 | tf_op jit(solution)/shard_map/reduce_scatter | solution.py:142
  158.8 4.7 %copy-start.5 = (f32[1024]{0:T(1024)S(1)}, f32[1024]{0:T(1024)}, u32[]{:S(2)}) copy-start(f32[1024]{0:T(1024)} %param.30) | copy-start | bytes 12292
Sparse Core Ops, SparseCore 0:
  83.0 64.5 all-gather.2
  167.2 30.1 reduce-scatter.1
where the time goes:
time: 205 us; the launch traced here: 204 us
  blocking collectives  107 us (52%)
  waiting for transfers between devices  30.3 us (15%)
  local copies, waits for them, and re-layouts  26.2 us (13%)
  matrix products  20.1 us (10%)
  between operations  14.4 us (7%)
  other arithmetic  5.74 us (3%)
    all_gather x1, blocking collectives, on_device(): lax.all_gather(query, 'seq', axis=0, tiled=True)  36.2 us
    all_gather x1, blocking collectives, on_device(): lax.all_gather(jnp.concatenate([slot_sum, long_sum], axis=0), 'seq', axis...  35.5 us
    all_gather x1, blocking collectives, on_device(): lax.all_gather(jnp.concatenate([slot_max, long_max], axis=0), 'seq', axis...  30.4 us
    reduce_scatter x1, waiting for transfers between devices, on_device(): lax.psum_scatter(partial_out.astype(jnp.bfloat16), 'tp', scatter_dimensio...  30.3 us
    reshape x1, local copies, waits for them, and re-layouts, page_terms(): shaped_keys = keys.reshape(page_count, cell_count, head_count, 2, DH)  9.36 us
    dot_general x2, matrix products, page_terms(): jnp.einsum('pchjd,phjd->pchj', shaped_keys, page_q, preferred_element_typ...  8.19 us
    dot_general x2, matrix products, page_terms(): jnp.einsum('pchj,pchv->phjv', weights.astype(jnp.bfloat16), shaped_values...  5.46 us
    unnamed x1, blocking collectives  5.28 us
  transfers between devices with their start and end apart: 2, of which 1 were waited for; matrix products, arithmetic and copies ran while one was open for 2% of the time, Pallas kernels for 0%

commit v1 on v0

v1 whole, which is shorter than its diff:
```python
import functools

import jax
import jax.numpy as jnp
from jax import lax
from jax.experimental import pallas as pl
from jax.experimental.pallas import tpu as pltpu
from jax.sharding import PartitionSpec as P

DH = 128
DV = 256
PG = 64
LANES = 128
ROWS = 16
MASKED = -1e30
MESH = pl.DeviceIdType.MESH


def split3(x):
    high = x.astype(jnp.bfloat16).astype(jnp.float32)
    rest = x - high
    mid = rest.astype(jnp.bfloat16).astype(jnp.float32)
    return high, mid, rest - mid


def lane_pack(lane, columns):
    packed = jnp.zeros(lane.shape, jnp.float32)
    for at, column in enumerate(columns):
        packed = jnp.where(lane == at, column, packed)
    return packed


def kernel(
    seq_count,
    tp_count,
    heads,
    table_ref,
    len_ref,
    slot_ref,
    offset_ref,
    long_request_ref,
    long_len_ref,
    lambda_ref,
    query_ref,
    new_key_ref,
    new_value_ref,
    gain_ref,
    key_ref,
    value_ref,
    long_key_ref,
    long_value_ref,
    weight_ref,
    out_ref,
    key_buf,
    value_buf,
    long_key_buf,
    long_value_buf,
    weight_buf,
    bias_buf,
    own_query,
    all_query,
    term_out,
    term_in,
    attn_out,
    attn_in,
    part_out,
    part_in,
    load_sem,
    query_send,
    query_recv,
    term_send,
    term_recv,
    attn_send,
    attn_recv,
    part_send,
    part_recv,
):
    me = lax.axis_index("seq")
    tp_me = lax.axis_index("tp")
    blocks = heads * 2 * DV // LANES
    groups = seq_count // blocks
    group = me // blocks
    block_me = me % blocks
    req_count = query_ref.shape[0]
    serve_count = table_ref.shape[0]
    page_count = slot_ref.shape[0]
    long_count = long_request_ref.shape[0]
    long_cells = long_key_ref.shape[1]
    pool_cells = page_count * PG
    out_cols = weight_ref.shape[1] // tp_count

    loads = []
    for h in range(heads):
        cols = pl.ds(h * 2 * DH, 2 * DH)
        row = []
        for at, (src, dst) in enumerate(
            (
                (key_ref, key_buf),
                (long_key_ref, long_key_buf),
                (value_ref, value_buf),
                (long_value_ref, long_value_buf),
            )
        ):
            row.append(
                pltpu.make_async_copy(src.at[:, :, cols], dst.at[h], load_sem.at[4 * h + at])
            )
        loads.append(row)
    weight_load = pltpu.make_async_copy(weight_ref, weight_buf, load_sem.at[4 * heads])

    barrier = pltpu.get_barrier_semaphore()
    for k in range(1, seq_count):
        pl.semaphore_signal(
            barrier, inc=1, device_id={"seq": lax.rem(me + k, seq_count)}, device_id_type=MESH
        )
    for k in range(1, tp_count):
        pl.semaphore_signal(
            barrier, inc=1, device_id={"tp": lax.rem(tp_me + k, tp_count)}, device_id_type=MESH
        )
    for row in loads:
        for copy in row:
            copy.start()
    weight_load.start()

    query = query_ref[...].astype(jnp.float32)
    half = query.shape[1] // 2
    own_query[...] = jnp.concatenate([query[:, :half], query[:, half:]], axis=0).astype(
        jnp.bfloat16
    )
    all_query[me] = own_query[...]
    pl.semaphore_wait(barrier, seq_count + tp_count - 2)

    def query_copy(target, owner, at):
        return pltpu.make_async_remote_copy(
            src_ref=own_query,
            dst_ref=all_query.at[owner],
            send_sem=query_send.at[at],
            recv_sem=query_recv.at[owner],
            device_id={"seq": target},
            device_id_type=MESH,
        )

    for k in range(1, seq_count):
        query_copy(lax.rem(me + k, seq_count), me, k - 1).start()

    lane = lax.broadcasted_iota(jnp.int32, (ROWS, LANES), 1)
    slot_row = lax.broadcasted_iota(jnp.int32, (ROWS, LANES), 0)
    length = jnp.zeros((ROWS, LANES), jnp.int32)
    owner = jnp.full((ROWS, LANES), -1, jnp.int32)
    for s in range(serve_count):
        length = jnp.where(slot_row == s, len_ref[s], length)
        owner = jnp.where(slot_row == s, table_ref[s], owner)
    for n in range(long_count):
        owner = jnp.where(slot_row == serve_count + n, long_request_ref[n], owner)
    per_chunk = LANES // PG
    for chunk in range(pool_cells // LANES):
        slot = jnp.full((ROWS, LANES), slot_ref[chunk * per_chunk], jnp.int32)
        offset = jnp.full((ROWS, LANES), offset_ref[chunk * per_chunk], jnp.int32)
        for extra in range(1, per_chunk):
            beyond = lane >= extra * PG
            slot = jnp.where(beyond, slot_ref[chunk * per_chunk + extra], slot)
            offset = jnp.where(beyond, offset_ref[chunk * per_chunk + extra], offset)
        live = (slot == slot_row) & (offset + (lane & (PG - 1)) < length)
        bias_buf[:, chunk * LANES : (chunk + 1) * LANES] = jnp.where(live, 0.0, MASKED)
    for n in range(long_count):
        for chunk in range(long_cells // LANES):
            pos = me * long_cells + chunk * LANES + lane
            live = (slot_row == serve_count + n) & (pos < long_len_ref[n])
            start = pool_cells + n * long_cells + chunk * LANES
            bias_buf[:, start : start + LANES] = jnp.where(live, 0.0, MASKED)

    products = query * new_key_ref[...].astype(jnp.float32)
    own_scores = [
        jnp.sum(products[:, m * DH : (m + 1) * DH], axis=1, keepdims=True) * DH ** (-0.5)
        for m in range(2 * heads)
    ]

    for k in range(1, seq_count):
        query_copy(me, lax.rem(me + seq_count - k, seq_count), k - 1).wait_recv()

    gathered = all_query[...].reshape(seq_count * ROWS, half)
    column = lax.broadcasted_iota(jnp.int32, (ROWS, seq_count * ROWS), 1)
    owner_wide = owner[:, :1]
    picks = []
    for part in range(2):
        local = (column & (ROWS - 1)) - part * req_count
        request = (column >> 4) * req_count + local
        hit = (local >= 0) & (local < req_count) & (request == owner_wide)
        pick = jnp.where(hit, 1.0, 0.0).astype(jnp.bfloat16)
        picks.append(jnp.dot(pick, gathered, preferred_element_type=jnp.float32))
    slot_query = jnp.concatenate(picks, axis=1)

    code = owner + 1
    id_high = (code >> 4).astype(jnp.float32)
    id_low = (code & 15).astype(jnp.float32)

    def term_copy(block, target, source):
        return pltpu.make_async_remote_copy(
            src_ref=term_out.at[block],
            dst_ref=term_in.at[source],
            send_sem=term_send.at[target],
            recv_sem=term_recv.at[source],
            device_id={"seq": target},
            device_id_type=MESH,
        )

    contract_last = (((1,), (1,)), ((), ()))
    for h in range(heads):
        maps = slot_query[:, h * 2 * DH : (h + 1) * 2 * DH]
        blank = jnp.zeros((ROWS, DH), jnp.float32)
        spread = jnp.concatenate(
            [
                jnp.concatenate([maps[:, :DH], blank], axis=1),
                jnp.concatenate([blank, maps[:, DH:]], axis=1),
            ],
            axis=0,
        ).astype(jnp.bfloat16)
        loads[h][0].wait()
        loads[h][1].wait()
        pool_scores = lax.dot_general(
            spread,
            key_buf[h].reshape(pool_cells, 2 * DH),
            contract_last,
            preferred_element_type=jnp.float32,
        )
        long_scores = lax.dot_general(
            spread,
            long_key_buf[h].reshape(long_count * long_cells, 2 * DH),
            contract_last,
            preferred_element_type=jnp.float32,
        )
        bias = bias_buf[...]
        bias = jnp.concatenate([bias, bias], axis=0)
        pool_scores = pool_scores * DH ** (-0.5) + bias[:, :pool_cells]
        long_scores = long_scores * DH ** (-0.5) + bias[:, pool_cells:]
        best = jnp.maximum(
            jnp.max(pool_scores, axis=1, keepdims=True),
            jnp.max(long_scores, axis=1, keepdims=True),
        )
        pool_w = jnp.exp(pool_scores - best)
        long_w = jnp.exp(long_scores - best)
        total = jnp.sum(pool_w, axis=1, keepdims=True) + jnp.sum(long_w, axis=1, keepdims=True)
        loads[h][2].wait()
        loads[h][3].wait()
        numer = jnp.dot(
            pool_w.astype(jnp.bfloat16),
            value_buf[h].reshape(pool_cells, DV),
            preferred_element_type=jnp.float32,
        ) + jnp.dot(
            long_w.astype(jnp.bfloat16),
            long_value_buf[h].reshape(long_count * long_cells, DV),
            preferred_element_type=jnp.float32,
        )
        some = best > 0.5 * MASKED
        mean = jnp.where(some, numer / total, 0.0)
        level = jnp.where(some, best + jnp.log(total), MASKED)
        for j in range(2):
            rows = slice(j * ROWS, (j + 1) * ROWS)
            meta = lane_pack(lane, (*split3(level[rows]), id_high, id_low))
            for c in range(2):
                block = (h * 2 + j) * 2 + c
                term_out[block] = jnp.concatenate(
                    [mean[rows, c * LANES : (c + 1) * LANES], meta], axis=0
                ).astype(jnp.bfloat16)
                for g in range(groups):
                    target = g * blocks + block

                    @pl.when(me != target)
                    def _():
                        term_copy(block, target, me).start()

                    @pl.when(me == target)
                    def _():
                        term_in[target] = term_out[block]

    for k in range(1, seq_count):
        source = lax.rem(me + seq_count - k, seq_count)
        term_copy(0, me, source).wait_recv()

    terms = term_in[...]
    means = terms[:, :ROWS].reshape(seq_count * ROWS, LANES)
    meta = jnp.transpose(terms[:, ROWS:].reshape(seq_count * ROWS, LANES).astype(jnp.float32))
    level = (meta[2:3] + meta[1:2]) + meta[0:1]
    ids = (meta[3:4] * 16.0 + meta[4:5]).astype(jnp.int32) - 1
    handled = blocks * req_count
    request = group * handled + lax.broadcasted_iota(
        jnp.int32, (handled, seq_count * ROWS), 0
    )
    member = request == ids
    top = jnp.max(jnp.where(member, level, MASKED), axis=1, keepdims=True)
    factor = jnp.where(member, jnp.exp(jnp.where(member, level - top, 0.0)), 0.0)
    total = jnp.sum(factor, axis=1, keepdims=True)
    high = factor.astype(jnp.bfloat16)
    low = (factor - high.astype(jnp.float32)).astype(jnp.bfloat16)
    merged = jnp.dot(high, means, preferred_element_type=jnp.float32) + jnp.dot(
        low, means, preferred_element_type=jnp.float32
    )
    some = total > 0.0
    safe = jnp.where(some, total, 1.0)
    merged = merged / safe
    level = jnp.where(some, top + jnp.log(safe), MASKED)
    wide = lax.broadcasted_iota(jnp.int32, (handled, LANES), 1)
    meta = lane_pack(wide, split3(level))
    attn_out[...] = jnp.concatenate(
        [
            merged.reshape(blocks, req_count, LANES),
            meta.reshape(blocks, req_count, LANES),
        ],
        axis=1,
    ).astype(jnp.bfloat16)

    def attn_copy(home, source_block):
        return pltpu.make_async_remote_copy(
            src_ref=attn_out.at[home],
            dst_ref=attn_in.at[source_block],
            send_sem=attn_send.at[home],
            recv_sem=attn_recv.at[source_block],
            device_id={"seq": group * blocks + home},
            device_id_type=MESH,
        )

    for k in range(1, blocks):
        attn_copy(lax.rem(block_me + k, blocks), block_me).start()
    attn_in[block_me] = attn_out[block_me]
    weight_load.wait()
    for k in range(1, blocks):
        attn_copy(block_me, lax.rem(block_me + blocks - k, blocks)).wait_recv()

    value = new_value_ref[...].astype(jnp.float32)
    normed = []
    for h in range(heads):
        diffs = []
        for c in range(2):
            attn = []
            for j in range(2):
                got = attn_in[(h * 2 + j) * 2 + c].astype(jnp.float32)
                info = got[req_count:]
                level = (info[:, 2:3] + info[:, 1:2]) + info[:, 0:1]
                score = own_scores[2 * h + j]
                top = jnp.maximum(score, level)
                own_w = jnp.exp(score - top)
                kept_w = jnp.exp(level - top)
                at = h * DV + c * LANES
                attn.append(
                    (own_w * value[:, at : at + LANES] + kept_w * got[:req_count])
                    / (own_w + kept_w)
                )
            diffs.append(attn[0] - lambda_ref[h] * attn[1])
        diff = jnp.concatenate(diffs, axis=1)
        square = jnp.sum(diff * diff, axis=1, keepdims=True) * (1.0 / DV)
        normed.append(
            diff * lax.rsqrt(square + 1e-05) * gain_ref[:, h * DV : (h + 1) * DV]
        )
    normed = jnp.concatenate(normed, axis=1).astype(jnp.bfloat16)

    def part_copy(target, source):
        return pltpu.make_async_remote_copy(
            src_ref=part_out.at[target],
            dst_ref=part_in.at[source],
            send_sem=part_send.at[target],
            recv_sem=part_recv.at[source],
            device_id={"tp": target},
            device_id_type=MESH,
        )

    def partial_out(target):
        cols = pl.ds(pl.multiple_of(target * out_cols, LANES), out_cols)
        return jnp.dot(normed, weight_buf[:, cols], preferred_element_type=jnp.float32)

    for k in range(1, tp_count):
        target = lax.rem(tp_me + k, tp_count)
        part_out[target] = partial_out(target)
        part_copy(target, tp_me).start()
    result = partial_out(tp_me)
    for k in range(1, tp_count):
        source = lax.rem(tp_me + tp_count - k, tp_count)
        part_copy(tp_me, source).wait_recv()
        result = result + part_in[source]
    out_ref[...] = result.astype(jnp.bfloat16)

    for k in range(1, seq_count):
        query_copy(lax.rem(me + k, seq_count), me, k - 1).wait_send()
        term_copy(0, lax.rem(me + k, seq_count), me).wait_send()
    for k in range(1, blocks):
        attn_copy(lax.rem(block_me + k, blocks), block_me).wait_send()
    for k in range(1, tp_count):
        part_copy(lax.rem(tp_me + k, tp_count), tp_me).wait_send()


def on_device(
    seq_count,
    tp_count,
    query,
    new_key,
    new_value,
    key_pool,
    value_pool,
    long_key,
    long_value,
    serve_table,
    serve_len,
    page_slot,
    page_offset,
    long_request,
    long_len,
    lambda_head,
    norm_gain,
    out_weight,
):
    heads = lambda_head.shape[0]
    req_count = query.shape[0]
    blocks = heads * 2 * DV // LANES
    pages = key_pool.shape[0]
    long_count, long_cells = long_key.shape[:2]
    out_cols = out_weight.shape[1] // tp_count
    cells = pages * PG + long_count * long_cells
    smem = pl.BlockSpec(memory_space=pltpu.SMEM)
    vmem = pl.BlockSpec(memory_space=pltpu.VMEM)
    hbm = pl.BlockSpec(memory_space=pl.ANY)
    bf16, f32 = jnp.bfloat16, jnp.float32
    dma = pltpu.SemaphoreType.DMA
    return pl.pallas_call(
        functools.partial(kernel, seq_count, tp_count, heads),
        out_shape=jax.ShapeDtypeStruct((req_count, out_cols), bf16),
        in_specs=[smem] * 7 + [vmem] * 4 + [hbm] * 5,
        out_specs=vmem,
        scratch_shapes=[
            pltpu.VMEM((heads, pages, PG, 2 * DH), bf16),
            pltpu.VMEM((heads, pages, PG, DV), bf16),
            pltpu.VMEM((heads, long_count, long_cells, 2 * DH), bf16),
            pltpu.VMEM((heads, long_count, long_cells, DV), bf16),
            pltpu.VMEM(out_weight.shape, bf16),
            pltpu.VMEM((ROWS, cells), f32),
            pltpu.VMEM((2 * req_count, query.shape[1] // 2), bf16),
            pltpu.VMEM((seq_count, 2 * req_count, query.shape[1] // 2), bf16),
            pltpu.VMEM((blocks, 2 * ROWS, LANES), bf16),
            pltpu.VMEM((seq_count, 2 * ROWS, LANES), bf16),
            pltpu.VMEM((blocks, 2 * req_count, LANES), bf16),
            pltpu.VMEM((blocks, 2 * req_count, LANES), bf16),
            pltpu.VMEM((tp_count, req_count, out_cols), f32),
            pltpu.VMEM((tp_count, req_count, out_cols), f32),
            dma((4 * heads + 1,)),
            dma((seq_count,)),
            dma((seq_count,)),
            dma((seq_count,)),
            dma((seq_count,)),
            dma((blocks,)),
            dma((blocks,)),
            dma((tp_count,)),
            dma((tp_count,)),
        ],
        compiler_params=pltpu.CompilerParams(
            collective_id=0, has_side_effects=True, vmem_limit_bytes=48 * 1024 * 1024
        ),
        cost_estimate=pl.CostEstimate(
            flops=4 * 32 * cells * heads * DV + 2 * req_count * out_weight.size,
            bytes_accessed=4 * (key_pool.size + long_key.size) + 2 * out_weight.size,
            transcendentals=32 * cells * heads,
        ),
        name="decode",
    )(
        serve_table,
        serve_len,
        page_slot,
        page_offset,
        long_request,
        long_len,
        lambda_head,
        query,
        new_key,
        new_value,
        norm_gain.reshape(1, -1),
        key_pool,
        value_pool,
        long_key,
        long_value,
        out_weight,
    )


def solution(mesh):
    return jax.shard_map(
        functools.partial(on_device, mesh.shape["seq"], mesh.shape["tp"]),
        mesh=mesh,
        in_specs=(
            P("seq", "tp"),
            P("seq", "tp"),
            P("seq", "tp"),
            P("seq", None, "tp"),
            P("seq", None, "tp"),
            P(None, "seq", "tp"),
            P(None, "seq", "tp"),
            P("seq"),
            P("seq"),
            P("seq"),
            P("seq"),
            P(),
            P(),
            P("tp"),
            P("tp"),
            P("tp", None),
        ),
        out_specs=P("seq", "tp"),
        check_vma=False,
    )
```

time: 205 us -> 44.6 us (0.22)
  blocking collectives: 107 us -> 0 us
  Pallas kernels: 0 us -> 32.9 us
  waiting for transfers between devices: 30.3 us -> 0 us
  matrix products: 20.1 us -> 0 us
  local copies, waits for them, and re-layouts: 26.2 us -> 11.2 us
  between operations: 14.4 us -> 0.02 us
  other arithmetic: 5.74 us -> 0 us
    all_gather x3 -> x0, blocking collectives: 102 us -> none  [the longest x1 36.2 us: on_device(): lax.all_gather(query, 'seq', axis=0, tiled=True)]
    pallas_call x0 -> x1, Pallas kernels: none -> 32.9 us  [on_device(): pl.pallas_call(functools.partial(kernel, seq_count, tp_count, heads), out...]
    reduce_scatter x1 -> x0, waiting for transfers between devices: 30.3 us -> none  [on_device(): lax.psum_scatter(partial_out.astype(jnp.bfloat16), 'tp', scatter_dimensio...]
    dot_general x11 -> x0, matrix products: 20.1 us -> none  [the longest x2 8.19 us: page_terms(): jnp.einsum('pchjd,phjd->pchj', shaped_keys, page_q, preferred_element_typ...]
    reshape x4 -> x0, local copies, waits for them, and re-layouts: 12.5 us -> none  [the longest x1 9.36 us: page_terms(): shaped_keys = keys.reshape(page_count, cell_count, head_count, 2, DH)]
    unnamed x28 -> x27, local copies, waits for them, and re-layouts: 1.71 us -> 11.2 us
    another operation x2 -> x0, local copies, waits for them, and re-layouts: 7.23 us -> none  [the longest x1 4.45 us: page_terms(): shaped_keys = keys.reshape(page_count, cell_count, head_count, 2, DH)]
    unnamed x1 -> x0, blocking collectives: 5.28 us -> none
  transfers between devices with their start and end apart: 2 -> 0, of which waited for: 1 -> 0; matrix products, arithmetic and copies ran while one was open for 2% -> 0% of each run, Pallas kernels for 0% -> 0%
where the time goes in v1:
time: 44.6 us; the launch traced here: 44.1 us
  Pallas kernels  32.9 us (74%)
  local copies, waits for them, and re-layouts  11.2 us (25%)
    pallas_call x1, Pallas kernels, on_device(): pl.pallas_call(functools.partial(kernel, seq_count, tp_count, heads), out...  32.9 us
    unnamed x27, local copies, waits for them, and re-layouts  11.2 us

profile of v1, /device:TPU:1, one launch (start us, length us, event | category | flops | bytes accessed | tf_op | source)
XLA Modules:
  0.0 44.1 jit_solution(977305077572366421)
XLA Ops:
  0.0 0.0 copy-start
  0.0 1.6 %copy-done = bf16[4,256,1024]{2,1,0:T(8,128)(2,1)S(1)} copy-done((bf16[4,256,1024]{2,1,0:T(8,128)(2,1)S(1)}, bf16[4,256,1024]{2,1,0:T(8,128)(2,1)}, u32[]{:S(2)}) %copy-start) | copy-done | bytes 2097176
  1.6 0.0 copy-start.1
  1.6 1.6 %copy-done.1 = bf16[4,256,1024]{2,1,0:T(8,128)(2,1)S(1)} copy-done((bf16[4,256,1024]{2,1,0:T(8,128)(2,1)S(1)}, bf16[4,256,1024]{2,1,0:T(8,128)(2,1)}, u32[]{:S(2)}) %copy-start.1) | copy-done | bytes 2097176
  3.2 0.0 copy-start.2
  3.2 0.7 %copy-done.2 = bf16[8,1024]{1,0:T(8,128)(2,1)S(1)} copy-done((bf16[8,1024]{1,0:T(8,128)(2,1)S(1)}, bf16[8,1024]{1,0:T(8,128)(2,1)}, u32[]{:S(2)}) %copy-start.2) | copy-done | bytes 16408
  3.9 0.0 copy-start.3
  3.9 0.7 %copy-done.3 = bf16[8,1024]{1,0:T(8,128)(2,1)S(1)} copy-done((bf16[8,1024]{1,0:T(8,128)(2,1)S(1)}, bf16[8,1024]{1,0:T(8,128)(2,1)}, u32[]{:S(2)}) %copy-start.3) | copy-done | bytes 16408
  4.6 0.0 copy-start.4
  4.6 0.7 %copy-done.4 = bf16[8,1024]{1,0:T(8,128)(2,1)S(1)} copy-done((bf16[8,1024]{1,0:T(8,128)(2,1)S(1)}, bf16[8,1024]{1,0:T(8,128)(2,1)}, u32[]{:S(2)}) %copy-start.4) | copy-done | bytes 16408
  5.3 0.0 copy-start.5
  5.3 0.7 %copy-done.5 = f32[1024]{0:T(1024)S(1)} copy-done((f32[1024]{0:T(1024)S(1)}, f32[1024]{0:T(1024)}, u32[]{:S(2)}) %copy-start.5) | copy-done | bytes 4120
  6.0 0.0 copy-start.6
  6.0 0.7 %copy-done.6 = s32[10]{0:T(128)S(1)} copy-done((s32[10]{0:T(128)S(1)}, s32[10]{0:T(128)}, u32[]{:S(2)}) %copy-start.6) | copy-done | bytes 64
  6.7 0.0 copy-start.7
  6.7 0.7 %copy-done.7 = s32[10]{0:T(128)S(1)} copy-done((s32[10]{0:T(128)S(1)}, s32[10]{0:T(128)}, u32[]{:S(2)}) %copy-start.7) | copy-done | bytes 64
  7.3 0.0 copy-start.8
  7.3 0.7 %copy-done.8 = s32[40]{0:T(128)S(1)} copy-done((s32[40]{0:T(128)S(1)}, s32[40]{0:T(128)}, u32[]{:S(2)}) %copy-start.8) | copy-done | bytes 184
  8.0 0.0 copy-start.9
  8.0 0.7 %copy-done.9 = s32[40]{0:T(128)S(1)} copy-done((s32[40]{0:T(128)S(1)}, s32[40]{0:T(128)}, u32[]{:S(2)}) %copy-start.9) | copy-done | bytes 184
  8.6 0.0 copy-start.10
  8.7 0.7 %copy-done.10 = s32[4]{0:T(128)S(1)} copy-done((s32[4]{0:T(128)S(1)}, s32[4]{0:T(128)}, u32[]{:S(2)}) %copy-start.10) | copy-done | bytes 40
  9.3 0.0 copy-start.11
  9.3 0.7 %copy-done.11 = s32[4]{0:T(128)S(1)} copy-done((s32[4]{0:T(128)S(1)}, s32[4]{0:T(128)}, u32[]{:S(2)}) %copy-start.11) | copy-done | bytes 40
  10.0 0.0 copy-start.12
  10.0 0.7 %copy-done.12 = f32[4]{0:T(128)S(1)} copy-done((f32[4]{0:T(128)S(1)}, f32[4]{0:T(128)}, u32[]{:S(2)}) %copy-start.12) | copy-done | bytes 40
  10.6 32.9 %decode.1 = bf16[8,1024]{1,0:T(8,128)(2,1)S(1)} custom-call(s32[10]{0:T(128)S(1)} %copy-done.6, s32[10]{0:T(128)S(1)} %copy-done.7, s32[40]{0:T(128)S(1)} %copy-done.8, s32[40]{0:T(128)S(1)} %copy-done.9, s32[4]{0:T(128)S(1)} %copy-done.10, s32[4]{0:T(128)S(1)} %copy-done.11, f32[4]{0:T(128)S(1)} %copy-done.12, bf16[8,1024]{1,0:T(8,128)(2,1)S(1)} %copy-done.2, ...), custom_call_target="tpu_custom_call" | custom-call | flops 503316480 | bytes 18874368 | tf_op jit(solution)/shard_map/decode/pallas_call | solution.py:421
  43.5 0.6 %copy.18 = bf16[8,1024]{1,0:T(8,128)(2,1)} copy(bf16[8,1024]{1,0:T(8,128)(2,1)S(1)} %decode.1) | data formatting | bytes 32768
Async XLA Ops:
  0.0 1.6 %copy-start = (bf16[4,256,1024]{2,1,0:T(8,128)(2,1)S(1)}, bf16[4,256,1024]{2,1,0:T(8,128)(2,1)}, u32[]{:S(2)}) copy-start(bf16[4,256,1024]{2,1,0:T(8,128)(2,1)} %long_key_ref.1) | copy-start | bytes 6291460
  1.6 1.6 %copy-start.1 = (bf16[4,256,1024]{2,1,0:T(8,128)(2,1)S(1)}, bf16[4,256,1024]{2,1,0:T(8,128)(2,1)}, u32[]{:S(2)}) copy-start(bf16[4,256,1024]{2,1,0:T(8,128)(2,1)} %long_value_ref.1) | copy-start | bytes 6291460
  3.2 0.7 %copy-start.2 = (bf16[8,1024]{1,0:T(8,128)(2,1)S(1)}, bf16[8,1024]{1,0:T(8,128)(2,1)}, u32[]{:S(2)}) copy-start(bf16[8,1024]{1,0:T(8,128)(2,1)} %query_ref.1) | copy-start | bytes 49156
  3.9 0.7 %copy-start.3 = (bf16[8,1024]{1,0:T(8,128)(2,1)S(1)}, bf16[8,1024]{1,0:T(8,128)(2,1)}, u32[]{:S(2)}) copy-start(bf16[8,1024]{1,0:T(8,128)(2,1)} %new_key_ref.1) | copy-start | bytes 49156
  4.6 0.7 %copy-start.4 = (bf16[8,1024]{1,0:T(8,128)(2,1)S(1)}, bf16[8,1024]{1,0:T(8,128)(2,1)}, u32[]{:S(2)}) copy-start(bf16[8,1024]{1,0:T(8,128)(2,1)} %new_value_ref.1) | copy-start | bytes 49156
  5.3 0.7 %copy-start.5 = (f32[1024]{0:T(1024)S(1)}, f32[1024]{0:T(1024)}, u32[]{:S(2)}) copy-start(f32[1024]{0:T(1024)} %param.30) | copy-start | bytes 12292
  6.0 0.7 %copy-start.6 = (s32[10]{0:T(128)S(1)}, s32[10]{0:T(128)}, u32[]{:S(2)}) copy-start(s32[10]{0:T(128)} %table_ref.1) | copy-start | bytes 124
  6.7 0.7 %copy-start.7 = (s32[10]{0:T(128)S(1)}, s32[10]{0:T(128)}, u32[]{:S(2)}) copy-start(s32[10]{0:T(128)} %len_ref.1) | copy-start | bytes 124
  7.3 0.7 %copy-start.8 = (s32[40]{0:T(128)S(1)}, s32[40]{0:T(128)}, u32[]{:S(2)}) copy-start(s32[40]{0:T(128)} %slot_ref.1) | copy-start | bytes 484
  8.0 0.7 %copy-start.9 = (s32[40]{0:T(128)S(1)}, s32[40]{0:T(128)}, u32[]{:S(2)}) copy-start(s32[40]{0:T(128)} %offset_ref.1) | copy-start | bytes 484
  8.6 0.7 %copy-start.10 = (s32[4]{0:T(128)S(1)}, s32[4]{0:T(128)}, u32[]{:S(2)}) copy-start(s32[4]{0:T(128)} %long_request_ref.1) | copy-start | bytes 52
  9.3 0.7 %copy-start.11 = (s32[4]{0:T(128)S(1)}, s32[4]{0:T(128)}, u32[]{:S(2)}) copy-start(s32[4]{0:T(128)} %long_len_ref.1) | copy-start | bytes 52
  10.0 0.7 %copy-start.12 = (f32[4]{0:T(128)S(1)}, f32[4]{0:T(128)}, u32[]{:S(2)}) copy-start(f32[4]{0:T(128)} %lambda_ref.1) | copy-start | bytes 52

commit v2 on v1

--- a/solution.py
+++ b/solution.py
@@ -34,6 +34,23 @@
     seq_count,
     tp_count,
     heads,
+    table_hbm,
+    len_hbm,
+    slot_hbm,
+    offset_hbm,
+    long_request_hbm,
+    long_len_hbm,
+    lambda_hbm,
+    query_hbm,
+    new_key_hbm,
+    new_value_hbm,
+    gain_hbm,
+    key_ref,
+    value_ref,
+    long_key_ref,
+    long_value_ref,
+    weight_ref,
+    out_ref,
     table_ref,
     len_ref,
     slot_ref,
@@ -45,12 +62,6 @@
     new_key_ref,
     new_value_ref,
     gain_ref,
-    key_ref,
-    value_ref,
-    long_key_ref,
-    long_value_ref,
-    weight_ref,
-    out_ref,
     key_buf,
     value_buf,
     long_key_buf,
@@ -74,11 +85,11 @@
     attn_recv,
     part_send,
     part_recv,
+    small_sem,
 ):
     me = lax.axis_index("seq")
     tp_me = lax.axis_index("tp")
     blocks = heads * 2 * DV // LANES
-    groups = seq_count // blocks
     group = me // blocks
     block_me = me % blocks
     req_count = query_ref.shape[0]
@@ -107,6 +118,25 @@
         loads.append(row)
     weight_load = pltpu.make_async_copy(weight_ref, weight_buf, load_sem.at[4 * heads])
 
+    smalls = [
+        pltpu.make_async_copy(src, dst, small_sem.at[at])
+        for at, (src, dst) in enumerate(
+            (
+                (query_hbm, query_ref),
+                (table_hbm, table_ref),
+                (len_hbm, len_ref),
+                (slot_hbm, slot_ref),
+                (offset_hbm, offset_ref),
+                (long_request_hbm, long_request_ref),
+                (long_len_hbm, long_len_ref),
+                (new_key_hbm, new_key_ref),
+                (lambda_hbm, lambda_ref),
+                (new_value_hbm, new_value_ref),
+                (gain_hbm, gain_ref),
+            )
+        )
+    ]
+    smalls[0].start()
     barrier = pltpu.get_barrier_semaphore()
     for k in range(1, seq_count):
         pl.semaphore_signal(
@@ -116,10 +146,12 @@
         pl.semaphore_signal(
             barrier, inc=1, device_id={"tp": lax.rem(tp_me + k, tp_count)}, device_id_type=MESH
         )
+    for copy in smalls[1:]:
+        copy.start()
     for row in loads:
-        for copy in row:
-            copy.start()
-    weight_load.start()
+        row[0].start()
+        row[1].start()
+    smalls[0].wait()
 
     query = query_ref[...].astype(jnp.float32)
     half = query.shape[1] // 2
@@ -141,6 +173,13 @@
 
     for k in range(1, seq_count):
         query_copy(lax.rem(me + k, seq_count), me, k - 1).start()
+
+    for row in loads:
+        row[2].start()
+        row[3].start()
+    weight_load.start()
+    for copy in smalls[1:]:
+        copy.wait()
 
     lane = lax.broadcasted_iota(jnp.int32, (ROWS, LANES), 1)
     slot_row = lax.broadcasted_iota(jnp.int32, (ROWS, LANES), 0)
@@ -174,6 +213,9 @@
         for m in range(2 * heads)
     ]
 
+    for row in loads:
+        for copy in row:
+            copy.wait()
     for k in range(1, seq_count):
         query_copy(me, lax.rem(me + seq_count - k, seq_count), k - 1).wait_recv()
 
@@ -214,8 +256,6 @@
             ],
             axis=0,
         ).astype(jnp.bfloat16)
-        loads[h][0].wait()
-        loads[h][1].wait()
         pool_scores = lax.dot_general(
             spread,
             key_buf[h].reshape(pool_cells, 2 * DH),
@@ -239,8 +279,6 @@
         pool_w = jnp.exp(pool_scores - best)
         long_w = jnp.exp(long_scores - best)
         total = jnp.sum(pool_w, axis=1, keepdims=True) + jnp.sum(long_w, axis=1, keepdims=True)
-        loads[h][2].wait()
-        loads[h][3].wait()
         numer = jnp.dot(
             pool_w.astype(jnp.bfloat16),
             value_buf[h].reshape(pool_cells, DV),
@@ -261,17 +299,11 @@
                 term_out[block] = jnp.concatenate(
                     [mean[rows, c * LANES : (c + 1) * LANES], meta], axis=0
                 ).astype(jnp.bfloat16)
-                for g in range(groups):
-                    target = g * blocks + block
-
-                    @pl.when(me != target)
-                    def _():
-                        term_copy(block, target, me).start()
-
-                    @pl.when(me == target)
-                    def _():
-                        term_in[target] = term_out[block]
-
+
+    for k in range(1, seq_count):
+        target = lax.rem(me + k, seq_count)
+        term_copy(lax.rem(target, blocks), target, me).start()
+    term_in[me] = term_out[block_me]
     for k in range(1, seq_count):
         source = lax.rem(me + seq_count - k, seq_count)
         term_copy(0, me, source).wait_recv()
@@ -413,7 +445,6 @@
     long_count, long_cells = long_key.shape[:2]
     out_cols = out_weight.shape[1] // tp_count
     cells = pages * PG + long_count * long_cells
-    smem = pl.BlockSpec(memory_space=pltpu.SMEM)
     vmem = pl.BlockSpec(memory_space=pltpu.VMEM)
     hbm = pl.BlockSpec(memory_space=pl.ANY)
     bf16, f32 = jnp.bfloat16, jnp.float32
@@ -421,9 +452,20 @@
     return pl.pallas_call(
         functools.partial(kernel, seq_count, tp_count, heads),
         out_shape=jax.ShapeDtypeStruct((req_count, out_cols), bf16),
-        in_specs=[smem] * 7 + [vmem] * 4 + [hbm] * 5,
+        in_specs=[hbm] * 16,
         out_specs=vmem,
         scratch_shapes=[
+            pltpu.SMEM(serve_table.shape, jnp.int32),
+            pltpu.SMEM(serve_len.shape, jnp.int32),
+            pltpu.SMEM(page_slot.shape, jnp.int32),
+            pltpu.SMEM(page_offset.shape, jnp.int32),
+            pltpu.SMEM(long_request.shape, jnp.int32),
+            pltpu.SMEM(long_len.shape, jnp.int32),
+            pltpu.SMEM(lambda_head.shape, f32),
+            pltpu.VMEM(query.shape, bf16),
+            pltpu.VMEM(new_key.shape, bf16),
+            pltpu.VMEM(new_value.shape, bf16),
+            pltpu.VMEM((1, norm_gain.size), f32),
             pltpu.VMEM((heads, pages, PG, 2 * DH), bf16),
             pltpu.VMEM((heads, pages, PG, DV), bf16),
             pltpu.VMEM((heads, long_count, long_cells, 2 * DH), bf16),
@@ -447,9 +489,10 @@
             dma((blocks,)),
             dma((tp_count,)),
             dma((tp_count,)),
+            dma((11,)),
         ],
         compiler_params=pltpu.CompilerParams(
-            collective_id=0, has_side_effects=True, vmem_limit_bytes=48 * 1024 * 1024
+            collective_id=0, has_side_effects=True, vmem_limit_bytes=64 * 1024 * 1024
         ),
         cost_estimate=pl.CostEstimate(
             flops=4 * 32 * cells * heads * DV + 2 * req_count * out_weight.size,

time: 44.6 us -> 33.5 us (0.75)
  local copies, waits for them, and re-layouts: 11.2 us -> 1.32 us
  Pallas kernels: 32.9 us -> 31.8 us
    unnamed x27 -> x1, local copies, waits for them, and re-layouts: 11.2 us -> 1.32 us
    pallas_call x1, Pallas kernels: 32.9 us -> 31.8 us  [on_device(): pl.pallas_call(functools.partial(kernel, seq_count, tp_count, heads), out...]
where the time goes in v2:
time: 33.5 us; the launch traced here: 33.2 us
  Pallas kernels  31.8 us (95%)
  local copies, waits for them, and re-layouts  1.32 us (4%)
    pallas_call x1, Pallas kernels, on_device(): pl.pallas_call(functools.partial(kernel, seq_count, tp_count, heads), out...  31.8 us
    unnamed x1, local copies, waits for them, and re-layouts  1.32 us

profile of v2, /device:TPU:1, one launch (start us, length us, event | category | flops | bytes accessed | tf_op | source)
XLA Modules:
  0.0 33.2 jit_solution(8382094776531841324)
XLA Ops:
  0.0 31.8 %decode.1 = bf16[8,1024]{1,0:T(8,128)(2,1)} custom-call(s32[10]{0:T(128)} %table_hbm.1, s32[10]{0:T(128)} %len_hbm.1, s32[40]{0:T(128)} %slot_hbm.1, s32[40]{0:T(128)} %offset_hbm.1, s32[4]{0:T(128)} %long_request_hbm.1, s32[4]{0:T(128)} %long_len_hbm.1, f32[4]{0:T(128)} %lambda_hbm.1, bf16[8,1024]{1,0:T(8,128)(2,1)} %query_hbm.1, ...), custom_call_target="tpu_custom_call" | custom-call | flops 503316480 | bytes 18874368 | tf_op jit(solution)/shard_map/decode/pallas_call | solution.py:452
  31.8 1.3 %copy.18 = bf16[8,1024]{1,0:T(8,128)(2,1)} copy(bf16[8,1024]{1,0:T(8,128)(2,1)} %decode.1) | data formatting | bytes 32768

commit v3 on v2

--- a/solution.py
+++ b/solution.py
@@ -99,10 +99,14 @@
     long_cells = long_key_ref.shape[1]
     pool_cells = page_count * PG
     out_cols = weight_ref.shape[1] // tp_count
+    chunks = own_query.shape[0]
+    chunk_heads = heads // chunks
+    chunk_blocks = blocks // chunks
+    width = chunk_heads * DV
 
     loads = []
-    for h in range(heads):
-        cols = pl.ds(h * 2 * DH, 2 * DH)
+    for h in range(chunks):
+        cols = pl.ds(h * width, width)
         row = []
         for at, (src, dst) in enumerate(
             (
@@ -116,7 +120,7 @@
                 pltpu.make_async_copy(src.at[:, :, cols], dst.at[h], load_sem.at[4 * h + at])
             )
         loads.append(row)
-    weight_load = pltpu.make_async_copy(weight_ref, weight_buf, load_sem.at[4 * heads])
+    weight_load = pltpu.make_async_copy(weight_ref, weight_buf, load_sem.at[4 * chunks])
 
     smalls = [
         pltpu.make_async_copy(src, dst, small_sem.at[at])
@@ -148,35 +152,38 @@
         )
     for copy in smalls[1:]:
         copy.start()
-    for row in loads:
-        row[0].start()
-        row[1].start()
+    for copy in loads[0]:
+        copy.start()
     smalls[0].wait()
 
     query = query_ref[...].astype(jnp.float32)
-    half = query.shape[1] // 2
-    own_query[...] = jnp.concatenate([query[:, :half], query[:, half:]], axis=0).astype(
-        jnp.bfloat16
-    )
-    all_query[me] = own_query[...]
+    half = width // 2
+    for p in range(chunks):
+        at = p * width
+        packed = jnp.concatenate(
+            [query[:, at : at + half], query[:, at + half : at + width]], axis=0
+        ).astype(jnp.bfloat16)
+        own_query[p] = packed
+        all_query[p, me] = packed
     pl.semaphore_wait(barrier, seq_count + tp_count - 2)
 
-    def query_copy(target, owner, at):
+    def query_copy(p, target, owner, at):
         return pltpu.make_async_remote_copy(
-            src_ref=own_query,
-            dst_ref=all_query.at[owner],
-            send_sem=query_send.at[at],
-            recv_sem=query_recv.at[owner],
+            src_ref=own_query.at[p],
+            dst_ref=all_query.at[p, owner],
+            send_sem=query_send.at[p, at],
+            recv_sem=query_recv.at[p, owner],
             device_id={"seq": target},
             device_id_type=MESH,
         )
 
-    for k in range(1, seq_count):
-        query_copy(lax.rem(me + k, seq_count), me, k - 1).start()
-
-    for row in loads:
-        row[2].start()
-        row[3].start()
+    for p in range(chunks):
+        for k in range(1, seq_count):
+            query_copy(p, lax.rem(me + k, seq_count), me, k - 1).start()
+
+    for row in loads[1:]:
+        for copy in row:
+            copy.start()
     weight_load.start()
     for copy in smalls[1:]:
         copy.wait()
@@ -213,13 +220,6 @@
         for m in range(2 * heads)
     ]
 
-    for row in loads:
-        for copy in row:
-            copy.wait()
-    for k in range(1, seq_count):
-        query_copy(me, lax.rem(me + seq_count - k, seq_count), k - 1).wait_recv()
-
-    gathered = all_query[...].reshape(seq_count * ROWS, half)
     column = lax.broadcasted_iota(jnp.int32, (ROWS, seq_count * ROWS), 1)
     owner_wide = owner[:, :1]
     picks = []
@@ -227,9 +227,7 @@
         local = (column & (ROWS - 1)) - part * req_count
         request = (column >> 4) * req_count + local
         hit = (local >= 0) & (local < req_count) & (request == owner_wide)
-        pick = jnp.where(hit, 1.0, 0.0).astype(jnp.bfloat16)
-        picks.append(jnp.dot(pick, gathered, preferred_element_type=jnp.float32))
-    slot_query = jnp.concatenate(picks, axis=1)
+        picks.append(jnp.where(hit, 1.0, 0.0).astype(jnp.bfloat16))
 
     code = owner + 1
     id_high = (code >> 4).astype(jnp.float32)
@@ -247,7 +245,20 @@
 
     contract_last = (((1,), (1,)), ((), ()))
     for h in range(heads):
-        maps = slot_query[:, h * 2 * DH : (h + 1) * 2 * DH]
+        p, inner = h // chunk_heads, h % chunk_heads
+        lanes = slice(inner * DV, (inner + 1) * DV)
+        if inner == 0:
+            for copy in loads[p]:
+                copy.wait()
+            for k in range(1, seq_count):
+                source = lax.rem(me + seq_count - k, seq_count)
+                query_copy(p, me, source, k - 1).wait_recv()
+            gathered = all_query[p].reshape(seq_count * ROWS, half)
+            slot_query = jnp.concatenate(
+                [jnp.dot(pick, gathered, preferred_element_type=jnp.float32) for pick in picks],
+                axis=1,
+            )
+        maps = slot_query[:, lanes]
         blank = jnp.zeros((ROWS, DH), jnp.float32)
         spread = jnp.concatenate(
             [
@@ -258,13 +269,13 @@
         ).astype(jnp.bfloat16)
         pool_scores = lax.dot_general(
             spread,
-            key_buf[h].reshape(pool_cells, 2 * DH),
+            key_buf[p, :, :, lanes].reshape(pool_cells, 2 * DH),
             contract_last,
             preferred_element_type=jnp.float32,
         )
         long_scores = lax.dot_general(
             spread,
-            long_key_buf[h].reshape(long_count * long_cells, 2 * DH),
+            long_key_buf[p, :, :, lanes].reshape(long_count * long_cells, 2 * DH),
             contract_last,
             preferred_element_type=jnp.float32,
         )
@@ -281,11 +292,11 @@
         total = jnp.sum(pool_w, axis=1, keepdims=True) + jnp.sum(long_w, axis=1, keepdims=True)
         numer = jnp.dot(
             pool_w.astype(jnp.bfloat16),
-            value_buf[h].reshape(pool_cells, DV),
+            value_buf[p, :, :, lanes].reshape(pool_cells, DV),
             preferred_element_type=jnp.float32,
         ) + jnp.dot(
             long_w.astype(jnp.bfloat16),
-            long_value_buf[h].reshape(long_count * long_cells, DV),
+            long_value_buf[p, :, :, lanes].reshape(long_count * long_cells, DV),
             preferred_element_type=jnp.float32,
         )
         some = best > 0.5 * MASKED
@@ -299,10 +310,19 @@
                 term_out[block] = jnp.concatenate(
                     [mean[rows, c * LANES : (c + 1) * LANES], meta], axis=0
                 ).astype(jnp.bfloat16)
-
-    for k in range(1, seq_count):
-        target = lax.rem(me + k, seq_count)
-        term_copy(lax.rem(target, blocks), target, me).start()
+        if inner == chunk_heads - 1:
+            for g in range(seq_count // blocks):
+                for k in range(chunk_blocks):
+                    block = p * chunk_blocks + lax.rem(me + k, chunk_blocks)
+                    target = g * blocks + block
+                    if k:
+                        term_copy(block, target, me).start()
+                    else:
+
+                        @pl.when(target != me)
+                        def _():
+                            term_copy(block, target, me).start()
+
     term_in[me] = term_out[block_me]
     for k in range(1, seq_count):
         source = lax.rem(me + seq_count - k, seq_count)
@@ -410,7 +430,8 @@
     out_ref[...] = result.astype(jnp.bfloat16)
 
     for k in range(1, seq_count):
-        query_copy(lax.rem(me + k, seq_count), me, k - 1).wait_send()
+        for p in range(chunks):
+            query_copy(p, lax.rem(me + k, seq_count), me, k - 1).wait_send()
         term_copy(0, lax.rem(me + k, seq_count), me).wait_send()
     for k in range(1, blocks):
         attn_copy(lax.rem(block_me + k, blocks), block_me).wait_send()
@@ -444,6 +465,8 @@
     pages = key_pool.shape[0]
     long_count, long_cells = long_key.shape[:2]
     out_cols = out_weight.shape[1] // tp_count
+    chunks = 2 if heads % 2 == 0 else 1
+    width = heads // chunks * DV
     cells = pages * PG + long_count * long_cells
     vmem = pl.BlockSpec(memory_space=pltpu.VMEM)
     hbm = pl.BlockSpec(memory_space=pl.ANY)
@@ -466,23 +489,23 @@
             pltpu.VMEM(new_key.shape, bf16),
             pltpu.VMEM(new_value.shape, bf16),
             pltpu.VMEM((1, norm_gain.size), f32),
-            pltpu.VMEM((heads, pages, PG, 2 * DH), bf16),
-            pltpu.VMEM((heads, pages, PG, DV), bf16),
-            pltpu.VMEM((heads, long_count, long_cells, 2 * DH), bf16),
-            pltpu.VMEM((heads, long_count, long_cells, DV), bf16),
+            pltpu.VMEM((chunks, pages, PG, width), bf16),
+            pltpu.VMEM((chunks, pages, PG, width), bf16),
+            pltpu.VMEM((chunks, long_count, long_cells, width), bf16),
+            pltpu.VMEM((chunks, long_count, long_cells, width), bf16),
             pltpu.VMEM(out_weight.shape, bf16),
             pltpu.VMEM((ROWS, cells), f32),
-            pltpu.VMEM((2 * req_count, query.shape[1] // 2), bf16),
-            pltpu.VMEM((seq_count, 2 * req_count, query.shape[1] // 2), bf16),
+            pltpu.VMEM((chunks, 2 * req_count, width // 2), bf16),
+            pltpu.VMEM((chunks, seq_count, 2 * req_count, width // 2), bf16),
             pltpu.VMEM((blocks, 2 * ROWS, LANES), bf16),
             pltpu.VMEM((seq_count, 2 * ROWS, LANES), bf16),
             pltpu.VMEM((blocks, 2 * req_count, LANES), bf16),
             pltpu.VMEM((blocks, 2 * req_count, LANES), bf16),
             pltpu.VMEM((tp_count, req_count, out_cols), f32),
             pltpu.VMEM((tp_count, req_count, out_cols), f32),
-            dma((4 * heads + 1,)),
-            dma((seq_count,)),
-            dma((seq_count,)),
+            dma((4 * chunks + 1,)),
+            dma((chunks, seq_count)),
+            dma((chunks, seq_count)),
             dma((seq_count,)),
             dma((seq_count,)),
             dma((blocks,)),

time: 33.5 us -> 32.9 us (0.982)
  Pallas kernels: 31.8 us -> 31.3 us
    pallas_call x1, Pallas kernels: 31.8 us -> 31.3 us  [on_device(): pl.pallas_call(functools.partial(kernel, seq_count, tp_count, heads), out...]
where the time goes in v3:
time: 32.9 us; the launch traced here: 32.6 us
  Pallas kernels  31.3 us (95%)
  local copies, waits for them, and re-layouts  1.32 us (4%)
    pallas_call x1, Pallas kernels, on_device(): pl.pallas_call(functools.partial(kernel, seq_count, tp_count, heads), out...  31.3 us
    unnamed x1, local copies, waits for them, and re-layouts  1.32 us

profile of v3, /device:TPU:1, one launch (start us, length us, event | category | flops | bytes accessed | tf_op | source)
XLA Modules:
  0.0 32.6 jit_solution(16613419751320367429)
XLA Ops:
  0.0 31.3 %decode.1 = bf16[8,1024]{1,0:T(8,128)(2,1)} custom-call(s32[10]{0:T(128)} %table_hbm.1, s32[10]{0:T(128)} %len_hbm.1, s32[40]{0:T(128)} %slot_hbm.1, s32[40]{0:T(128)} %offset_hbm.1, s32[4]{0:T(128)} %long_request_hbm.1, s32[4]{0:T(128)} %long_len_hbm.1, f32[4]{0:T(128)} %lambda_hbm.1, bf16[8,1024]{1,0:T(8,128)(2,1)} %query_hbm.1, ...), custom_call_target="tpu_custom_call" | custom-call | flops 503316480 | bytes 18874368 | tf_op jit(solution)/shard_map/decode/pallas_call | solution.py:475
  31.3 1.3 %copy.18 = bf16[8,1024]{1,0:T(8,128)(2,1)} copy(bf16[8,1024]{1,0:T(8,128)(2,1)} %decode.1) | data formatting | bytes 32768

commit v4 on v3

--- a/solution.py
+++ b/solution.py
@@ -180,10 +180,10 @@
     for p in range(chunks):
         for k in range(1, seq_count):
             query_copy(p, lax.rem(me + k, seq_count), me, k - 1).start()
-
-    for row in loads[1:]:
-        for copy in row:
-            copy.start()
+        if p + 1 < chunks:
+            for copy in loads[p + 1]:
+                copy.start()
+
     weight_load.start()
     for copy in smalls[1:]:
         copy.wait()
@@ -465,7 +465,7 @@
     pages = key_pool.shape[0]
     long_count, long_cells = long_key.shape[:2]
     out_cols = out_weight.shape[1] // tp_count
-    chunks = 2 if heads % 2 == 0 else 1
+    chunks = heads
     width = heads // chunks * DV
     cells = pages * PG + long_count * long_cells
     vmem = pl.BlockSpec(memory_space=pltpu.VMEM)

time: 32.9 us -> 33 us (level)
  no operation moved by 1% of the time
where the time goes in v4:
time: 33 us; the launch traced here: 32.6 us
  Pallas kernels  31.3 us (95%)
  local copies, waits for them, and re-layouts  1.32 us (4%)
    pallas_call x1, Pallas kernels, on_device(): pl.pallas_call(functools.partial(kernel, seq_count, tp_count, heads), out...  31.3 us
    unnamed x1, local copies, waits for them, and re-layouts  1.32 us

profile of v4, /device:TPU:1, one launch (start us, length us, event | category | flops | bytes accessed | tf_op | source)
XLA Modules:
  0.0 32.6 jit_solution(8140390390241712042)
XLA Ops:
  0.0 31.3 %decode.1 = bf16[8,1024]{1,0:T(8,128)(2,1)} custom-call(s32[10]{0:T(128)} %table_hbm.1, s32[10]{0:T(128)} %len_hbm.1, s32[40]{0:T(128)} %slot_hbm.1, s32[40]{0:T(128)} %offset_hbm.1, s32[4]{0:T(128)} %long_request_hbm.1, s32[4]{0:T(128)} %long_len_hbm.1, f32[4]{0:T(128)} %lambda_hbm.1, bf16[8,1024]{1,0:T(8,128)(2,1)} %query_hbm.1, ...), custom_call_target="tpu_custom_call" | custom-call | flops 503316480 | bytes 18874368 | tf_op jit(solution)/shard_map/decode/pallas_call | solution.py:475
  31.3 1.3 %copy.18 = bf16[8,1024]{1,0:T(8,128)(2,1)} copy(bf16[8,1024]{1,0:T(8,128)(2,1)} %decode.1) | data formatting | bytes 32768
